TPU v7x, 128 devices: a whole 4x4x4 slice. The times are simulated.
128 devices in a mesh: grp: 2 (over x_lo), ctx: 64 (over x_hi, y, z, core).
Axes of the slice: x: 4 (x_hi: 2, x_lo: 2; x = x_hi * 2 + x_lo), y: 4, z: 4, core: 2. Of those that a mesh axis runs over, the one named last changes fastest.
Arguments:
- queries: bfloat16 [12288, 1536], P('ctx', 'grp'), may hold values from -9 to 9
- key_tokens: bfloat16 [12288, 1536], P('ctx', 'grp'), may hold values from -9 to 9
- value_tokens: bfloat16 [12288, 1536], P('ctx', 'grp'), may hold values from -6 to 6
- hidden: bfloat16 [12288, 1536], P('ctx'), may hold values from -6 to 6
- out_weight: bfloat16 [1536, 1536], replicated, may hold values from -0.15625 to 0.15625
- attn_gate: float32 [1536], replicated, may hold values from 0.5 to 2
Outputs:
- block_out: bfloat16 [12288, 1536], P('ctx')
All inputs are finite; a program needn't handle non-finite values.
Results may differ from a plain program's by a relative error of at most 0.009.
Values may be sent and summed in bfloat16 or wider, within the bound.
A program may use at most 192 MiB of HBM per device.

v0:
```python
import jax
import jax.numpy as jnp
from jax import lax
from jax.sharding import PartitionSpec as P

DH = 128


def on_device(queries, key_tokens, value_tokens, hidden, out_weight, attn_gate):
    tok_rows = queries.shape[0]
    local_feats = queries.shape[1]
    local_heads = local_feats // DH
    score_scale = DH ** (-0.5)
    query_heads = queries.reshape(tok_rows, local_heads, DH)
    key_all, value_all = (
        lax.all_gather(key_tokens, "ctx", axis=0, tiled=True),
        lax.all_gather(value_tokens, "ctx", axis=0, tiled=True),
    )
    key_heads = key_all.reshape(-1, local_heads, DH)
    value_heads = value_all.reshape(-1, local_heads, DH)
    half = local_heads // 2
    mixed_parts = []
    mass_parts = []
    for group in range(2):
        lo = group * half
        scores = (
            jnp.einsum(
                "thd,shd->hts",
                query_heads[:, lo : lo + half],
                key_heads[:, lo : lo + half],
                preferred_element_type=jnp.float32,
            )
            * score_scale
        )
        row_max = jnp.max(scores, axis=-1)
        weights = jnp.exp(scores - row_max[:, :, None])
        mass_parts.append(jnp.sum(weights, axis=-1))
        mixed_parts.append(
            jnp.einsum(
                "hts,shd->thd",
                weights.astype(jnp.bfloat16),
                value_heads[:, lo : lo + half],
                preferred_element_type=jnp.float32,
            )
        )
    mixed = jnp.concatenate(mixed_parts, axis=1)
    mass = jnp.concatenate(mass_parts, axis=0)
    attended = (
        (mixed / jnp.transpose(mass)[:, :, None])
        .reshape(tok_rows, local_feats)
        .astype(jnp.bfloat16)
    )
    start = lax.axis_index("grp") * local_feats
    rows_mine = lax.dynamic_slice_in_dim(out_weight, start, local_feats, 0)
    partial_proj = jnp.dot(attended, rows_mine, preferred_element_type=jnp.float32)
    projected = lax.psum(partial_proj.astype(jnp.bfloat16), "grp").astype(jnp.float32)
    return (hidden.astype(jnp.float32) + attn_gate * projected).astype(jnp.bfloat16)


def solution(mesh):
    return jax.shard_map(
        on_device,
        mesh=mesh,
        in_specs=(P("ctx", "grp"), P("ctx", "grp"), P("ctx", "grp"), P("ctx", None), P(), P()),
        out_specs=P("ctx", None),
        check_vma=False,
    )
```

profile of v0, /device:TPU:1, one launch (start us, length us, event | category | flops | bytes accessed | tf_op | source)
XLA Modules:
  0.0 363.4 jit_solution(14270717357782616307)
XLA Ops:
  6.5 0.0 all-gather.3.cloned.1.call-start
  6.5 0.7 all-gather.3.cloned.1.call-update
  7.3 0.0 all-gather.5.cloned.1.call-start
  7.3 0.7 all-gather.5.cloned.1.call-update
  8.0 0.0 all-reduce.2.cloned.1.call-start
  8.1 1.3 reshape.18
  9.4 0.1 fusion.38
  9.5 116.5 %all-gather.3.cloned.1.call-done = bf16[12288,768]{1,0:T(8,128)(2,1)} async-done(((bf16[192,768]{1,0:T(8,128)(2,1)}), bf16[12288,768]{1,0:T(8,128)(2,1)}) %all-gather.3.cloned.1.call-update) | async-done | bytes 18874384 | tf_op jit(solution)/shard_map/all_gather | solution.py:16
  126.0 24.7 %copy.17 = bf16[12288,768]{0,1:T(8,128)(2,1)} copy(bf16[12288,768]{1,0:T(8,128)(2,1)} %all-gather.3.cloned.1.call-done) | data formatting | bytes 37748736 | tf_op jit(solution)/shard_map/all_gather | solution.py:16
  150.7 13.9 %multiply_reduce_fusion.1 = (f32[3,192]{1,0:T(4,128)S(1)}, f32[3,192,12288]{2,1,0:T(8,128)}) fusion(bf16[12288,6,128]{0,2,1:T(8,128)(2,1)} %bitcast.15, bf16[192,3,128]{2,1,0:T(4,128)(2,1)S(1)} %get-tuple-element.5), kind=kOutput, calls=%fused_computation.3 | convolution fusion | flops 1826094592 | bytes 37898496 | tf_op jit(solution)/shard_map/thd,shd->hts/dot_general | solution.py:27
  164.6 13.9 %multiply_reduce_fusion = (f32[3,192]{1,0:T(4,128)S(1)}, f32[3,192,12288]{2,1,0:T(8,128)}) fusion(bf16[12288,6,128]{0,2,1:T(8,128)(2,1)} %bitcast.16, bf16[192,3,128]{2,1,0:T(4,128)(2,1)S(1)} %get-tuple-element.6), kind=kOutput, calls=%fused_computation.2 | convolution fusion | flops 1826094592 | bytes 37898496 | tf_op jit(solution)/shard_map/thd,shd->hts/dot_general | solution.py:27
  178.5 60.4 %all-gather.5.cloned.1.call-done = bf16[12288,768]{1,0:T(8,128)(2,1)} async-done(((bf16[192,768]{1,0:T(8,128)(2,1)}), bf16[12288,768]{1,0:T(8,128)(2,1)}) %all-gather.5.cloned.1.call-update) | async-done | bytes 18874384 | tf_op jit(solution)/shard_map/all_gather | solution.py:17
  238.8 24.5 %copy.19 = bf16[12288,768]{0,1:T(8,128)(2,1)} copy(bf16[12288,768]{1,0:T(8,128)(2,1)} %all-gather.5.cloned.1.call-done) | data formatting | bytes 37748736 | tf_op jit(solution)/shard_map/all_gather | solution.py:17
  263.3 17.0 %fusion.19 = f32[192,3,128]{2,0,1:T(8,128)S(1)} fusion(bf16[12288,6,128]{0,2,1:T(8,128)(2,1)} %bitcast.17, f32[3,192,12288]{2,1,0:T(8,128)} %get-tuple-element.10, f32[3,192]{1,0:T(4,128)S(1)} %get-tuple-element.9), kind=kOutput, calls=%fused_computation.23 | convolution fusion | flops 1833172992 | bytes 38045952 | tf_op jit(solution)/shard_map/hts,shd->thd/dot_general | solution.py:39
  280.4 19.9 %fusion = (f32[3,192]{1,0:T(4,128)S(1)}, f32[3,192]{1,0:T(4,128)S(1)}) fusion(f32[3,192,12288]{2,1,0:T(8,128)} %get-tuple-element.10, f32[3,192]{1,0:T(4,128)S(1)} %get-tuple-element.9, f32[3,192]{1,0:T(4,128)S(1)} %get-tuple-element.7, f32[3,192,12288]{2,1,0:T(8,128)} %get-tuple-element.8), kind=kLoop, calls=%fused_computation.4 | loop fusion | flops 42466176 | bytes 56632320 | tf_op jit(solution)/shard_map/reduce_sum | solution.py:37
  300.3 0.0 copy-start
  300.3 0.0 copy-start.1
  300.3 17.1 %fusion.24 = f32[192,3,128]{2,0,1:T(8,128)S(1)} fusion(bf16[12288,6,128]{0,2,1:T(8,128)(2,1)} %bitcast.18, f32[3,192,12288]{2,1,0:T(8,128)} %get-tuple-element.8, f32[3,192]{1,0:T(4,128)S(1)} %get-tuple-element.7), kind=kOutput, calls=%fused_computation.24 | convolution fusion | flops 1833172992 | bytes 38045952 | tf_op jit(solution)/shard_map/hts,shd->thd/dot_general | solution.py:39
  317.5 3.2 convolution_convert_fusion
  320.7 0.0 all-reduce.2.cloned.1.call-update
  320.7 34.2 %all-reduce.2.cloned.1.call-done = bf16[192,1536]{1,0:T(8,128)(2,1)} async-done(((bf16[192,1536]{1,0:T(8,128)(2,1)}), bf16[192,1536]{1,0:T(8,128)(2,1)}) %all-reduce.2.cloned.1.call-update) | async-done | bytes 589840 | tf_op jit(solution)/shard_map/psum | solution.py:56
  354.8 0.0 copy-done
  354.8 0.0 copy-done.1
  354.8 2.1 add_convert_fusion
  (1 shorter events, 0.0 us)
Async XLA Ops:
  6.5 119.5 %all-gather.3.cloned.1.call-start = ((), (), s32[]{:S(2)}) async-start(), calls=%async_computation | async-start | bytes 19169280 | tf_op jit(solution)/shard_map/all_gather | solution.py:16
  7.3 231.6 %all-gather.5.cloned.1.call-start = ((), (), s32[]{:S(2)}) async-start(), calls=%async_computation.1 | async-start | bytes 19169280 | tf_op jit(solution)/shard_map/all_gather | solution.py:17
  8.0 346.8 %all-reduce.2.cloned.1.call-start = ((), (), s32[]{:S(2)}) async-start(), calls=%async_computation.2 | async-start | bytes 1179648 | tf_op jit(solution)/shard_map/psum | solution.py:56
  300.3 54.6 %copy-start = (bf16[192,1536]{1,0:T(8,128)(2,1)S(1)}, bf16[192,1536]{1,0:T(8,128)(2,1)}, u32[]{:S(2)}) copy-start(bf16[192,1536]{1,0:T(8,128)(2,1)} %param.9) | copy-start | bytes 1769476
  300.3 54.6 %copy-start.1 = (f32[1536]{0:T(1024)S(1)}, f32[1536]{0:T(1024)}, u32[]{:S(2)}) copy-start(f32[1536]{0:T(1024)} %param.11) | copy-start | bytes 18436
Sparse Core Ops, SparseCore 0:
  10.5 115.4 all-gather.2
  129.2 109.6 all-gather.4
  320.8 33.9 all-reduce.1
where the time goes:
time: 365 us; the launch traced here: 363 us
  waiting for transfers between devices  212 us (58%)
  matrix products  65.2 us (18%)
  local copies, waits for them, and re-layouts  50.6 us (14%)
  other arithmetic  22 us (6%)
  between operations  13.2 us (4%)
    all_gather x1, waiting for transfers between devices, on_device(): lax.all_gather(key_tokens, 'ctx', axis=0, tiled=True)  116 us
    all_gather x1, waiting for transfers between devices, on_device(): lax.all_gather(value_tokens, 'ctx', axis=0, tiled=True)  60.4 us
    dot_general x2, matrix products, on_device(): jnp.einsum('hts,shd->thd', weights.astype(jnp.bfloat16), value_heads[:, l...  34.2 us
    psum x1, waiting for transfers between devices, on_device(): lax.psum(partial_proj.astype(jnp.bfloat16), 'grp').astype(jnp.float32)  34.2 us
    dot_general x2, matrix products, on_device(): jnp.einsum('thd,shd->hts', query_heads[:, lo:lo + half], key_heads[:, lo:...  27.8 us
    all_gather x1, local copies, waits for them, and re-layouts, on_device(): lax.all_gather(key_tokens, 'ctx', axis=0, tiled=True)  24.7 us
    all_gather x1, local copies, waits for them, and re-layouts, on_device(): lax.all_gather(value_tokens, 'ctx', axis=0, tiled=True)  24.5 us
    reduce_sum x1, other arithmetic, on_device(): mass_parts.append(jnp.sum(weights, axis=-1))  19.9 us
  transfers between devices with their start and end apart: 3, of which 3 were waited for; matrix products, arithmetic and copies ran while one was open for 15% of the time, Pallas kernels for 0%

commit v1 on v0

v1 whole, which is shorter than its diff:
```python
import jax
import jax.numpy as jnp
from jax import lax
from jax.experimental import pallas as pl
from jax.experimental.pallas import tpu as pltpu
from jax.sharding import PartitionSpec as P

DH = 128
TOK = 192
HEADS_DEV = 3
RING = 4
SCALE = DH**-0.5 * 1.4426950408889634
NT = (((1,), (1,)), ((), ()))
NN = (((1,), (0,)), ((), ()))
MESH = pl.DeviceIdType.MESH
KV_AXIS = ("y", "z", "y")
Q_AXIS = ("z", "y", "z")
PAIRS = ((1, 3), (2, 0))


def kernel(
    q_in, k_in, v_in, hidden_in, w_in, gate_ref, out_ref,
    kv, qb, o_send, o_recv, s_send, s_recv, att, a_send, w_buf, hid_buf,
    loc_sem, big_sem, x_send, x_recv, kv_send, kv_recv, q_send, q_recv,
    f_send, f_recv, o_ssem, o_rsem, s_ssem, s_rsem, a_ssem, a_rsem,
):
    g = lax.axis_index("grp")
    t = lax.axis_index("ctx")
    core = t % 2
    place = {"xh": t // 32, "y": (t // 8) % 4, "z": (t // 2) % 4, "core": core}
    xh = place["xh"]

    def device(grp=None, **moved):
        at = dict(place, **moved)
        ctx = ((at["xh"] * 4 + at["y"]) * 4 + at["z"]) * 2 + at["core"]
        return (g if grp is None else grp, ctx)

    def ring(axis, step):
        return device(**{axis: (place[axis] + step) % RING})

    sibling = device(core=1 - core)
    x_partner = device(xh=1 - xh)
    x_kinds = (device(grp=1 - g), x_partner, device(grp=1 - g, xh=1 - xh))

    def columns(half, h):
        return pl.ds(pl.multiple_of((half * HEADS_DEV + h) * DH, DH), DH)

    def remote(src, dst, send, recv, to):
        return pltpu.make_async_remote_copy(
            src_ref=src, dst_ref=dst, send_sem=send, recv_sem=recv, device_id=to, device_id_type=MESH
        )

    own = []
    for h in range(HEADS_DEV):
        cols = columns(xh, h)
        own.append((
            pltpu.make_async_copy(k_in.at[:, cols], kv.at[h, 0, 0, 0, :, pl.ds(0, DH)], loc_sem.at[h, 0]),
            pltpu.make_async_copy(v_in.at[:, cols], kv.at[h, 0, 0, 0, :, pl.ds(DH, DH)], loc_sem.at[h, 1]),
            pltpu.make_async_copy(q_in.at[:, cols], qb.at[h, 0, 0], loc_sem.at[h, 2]),
        ))
        for copy in own[h]:
            copy.start()
    w_copy = pltpu.make_async_copy(w_in, w_buf, big_sem.at[0])
    hid_copy = pltpu.make_async_copy(hidden_in, hid_buf, big_sem.at[1])
    w_copy.start()
    hid_copy.start()

    barrier = pltpu.get_barrier_semaphore()
    peers = [ring(a, s) for a in ("y", "z") for s in (1, 2, 3)] + [sibling, *x_kinds]
    for peer in peers:
        pl.semaphore_signal(barrier, inc=1, device_id=peer, device_id_type=MESH)
    pl.semaphore_wait(barrier, len(peers))

    sent = []

    def start(copy):
        copy.start()
        sent.append(copy)

    def x_copies(h):
        cols = columns(1 - xh, h)
        return [
            remote(k_in.at[:, cols], kv.at[h, 0, 1, 0, :, pl.ds(0, DH)], x_send.at[h, 0], x_recv.at[h, 0], x_partner),
            remote(v_in.at[:, cols], kv.at[h, 0, 1, 0, :, pl.ds(DH, DH)], x_send.at[h, 1], x_recv.at[h, 1], x_partner),
            remote(q_in.at[:, cols], qb.at[h, 0, 1], x_send.at[h, 2], x_recv.at[h, 2], x_partner),
        ]

    def kv_copy(h, xr, step):
        slot = RING - step
        return remote(
            kv.at[h, 0, xr, 0], kv.at[h, 0, xr, slot],
            kv_send.at[h, xr, slot - 1], kv_recv.at[h, xr, slot - 1], ring(KV_AXIS[h], step),
        )

    def q_copy(h, xr, step):
        slot = RING - step
        return remote(
            qb.at[h, 0, xr], qb.at[h, slot, xr],
            q_send.at[h, xr, slot - 1], q_recv.at[h, xr, slot - 1], ring(Q_AXIS[h], step),
        )

    def push(h, xr):
        for step in (2, 1, 3):
            start(kv_copy(h, xr, step))
        for step in (2, 1, 3):
            start(q_copy(h, xr, step))

    def forward_copy(h, xr):
        return remote(kv.at[h, 0, xr], kv.at[h, 1, xr], f_send.at[h, xr], f_recv.at[h, xr], sibling)

    for h in range(HEADS_DEV):
        for copy in x_copies(h):
            start(copy)
        for copy in own[h]:
            copy.wait()
        push(h, 0)
    for h in range(HEADS_DEV):
        for copy in x_copies(h):
            copy.wait_recv()
        push(h, 1)

    def gathered(h):
        for xr in range(2):
            for step in (1, 2, 3):
                kv_copy(h, xr, step).wait_recv()
            start(forward_copy(h, xr))
        for xr in range(2):
            for step in (1, 2, 3):
                q_copy(h, xr, step).wait_recv()

    def o_copies(h, d):
        slot = RING - d
        to = ring(Q_AXIS[h], d)
        return (
            remote(o_send.at[h, d], o_recv.at[h, slot - 1], o_ssem.at[h, slot - 1], o_rsem.at[h, slot - 1], to),
            remote(s_send.at[h, d], s_recv.at[h, slot - 1], s_ssem.at[h, slot - 1], s_rsem.at[h, slot - 1], to),
        )

    def attend(h, ds):
        blocks = [(cs, xr) for cs in range(2) for xr in range(2)]
        items = [(d, b) for d in ds for b in blocks]
        stacked = {}
        for d in ds:
            scaled = qb[h, d].reshape(2 * TOK, DH).astype(jnp.float32) * SCALE
            high = scaled.astype(jnp.bfloat16)
            low = (scaled - high.astype(jnp.float32)).astype(jnp.bfloat16)
            stacked[d] = jnp.concatenate([high, low], axis=1)

        def scores(item):
            d, (cs, xr) = item
            keys = kv[h, cs, xr, :, :, :DH].reshape(RING * TOK, DH)
            return lax.dot_general(
                stacked[d], jnp.concatenate([keys, keys], axis=1), NT, preferred_element_type=jnp.float32
            )

        state = {}
        ahead = scores(items[0])
        for n, (d, (cs, xr)) in enumerate(items):
            now = ahead
            if n + 1 < len(items):
                ahead = scores(items[n + 1])
            values = kv[h, cs, xr, :, :, DH:].reshape(RING * TOK, DH)
            top = jnp.max(now, axis=1, keepdims=True)
            if d in state:
                top = jnp.maximum(top, state[d][0])
            weights = jnp.exp2(now - top).astype(jnp.bfloat16)
            mixed = lax.dot_general(
                weights, jnp.concatenate([values, jnp.ones_like(values)], axis=1), NN,
                preferred_element_type=jnp.float32,
            )
            if d in state:
                mixed = mixed + state[d][1] * jnp.exp2(state[d][0] - top)
            state[d] = (top, mixed)
        for d in ds:
            top, mixed = state[d]
            mass = mixed[:, DH:]
            o_send[h, d] = (mixed[:, :DH] / mass).astype(jnp.bfloat16)
            s_send[h, d] = jnp.transpose(top + jnp.log2(mass))[:8]
        for d in ds:
            if d:
                for copy in o_copies(h, d):
                    start(copy)

    def a_copies(h):
        at = (g * 2 + xh) * HEADS_DEV + h
        return [
            remote(att.at[at] if kind == 0 else a_send.at[h], att.at[at], a_ssem.at[h, kind], a_rsem.at[h, kind], x_kinds[kind])
            for kind in range(3)
        ]

    def a_arrivals(h):
        places = ((1 - g) * 2 + xh, g * 2 + 1 - xh, (1 - g) * 2 + 1 - xh)
        return [
            remote(a_send.at[h], att.at[places[kind] * HEADS_DEV + h], a_ssem.at[h, kind], a_rsem.at[h, kind], x_kinds[kind])
            for kind in range(3)
        ]

    def combine(h):
        for d in (1, 2, 3):
            for copy in o_copies(h, d):
                copy.wait_recv()
        sums = [s_send[h, 0]] + [s_recv[h, j] for j in range(3)]
        parts = [o_send[h, 0]] + [o_recv[h, j] for j in range(3)]
        top = jnp.maximum(jnp.maximum(sums[0], sums[1]), jnp.maximum(sums[2], sums[3]))
        shares = [jnp.exp2(s - top) for s in sums]
        total = (shares[0] + shares[1]) + (shares[2] + shares[3])
        whole = None
        for share, part in zip(shares, parts):
            by_row = jnp.transpose(jnp.broadcast_to((share / total)[:1], (DH, 2 * TOK)))
            term = by_row * part.astype(jnp.float32)
            whole = term if whole is None else whole + term
        whole = whole.astype(jnp.bfloat16)
        att[(g * 2 + xh) * HEADS_DEV + h] = whole[:TOK]
        a_send[h] = whole[TOK:]
        for copy in a_copies(h):
            start(copy)

    for h in range(HEADS_DEV):
        gathered(h)
        for xr in range(2):
            forward_copy(h, xr).wait_recv()
        for ds in PAIRS:
            attend(h, ds)
        if h:
            combine(h - 1)
    combine(HEADS_DEV - 1)

    w_copy.wait()
    hid_copy.wait()
    for h in range(HEADS_DEV):
        for copy in a_arrivals(h):
            copy.wait_recv()
    pairs = [jnp.concatenate([att[2 * i], att[2 * i + 1]], axis=1) for i in range(6)]
    rows = jnp.concatenate(pairs, axis=1)

    def project(j, carry):
        cols = pl.ds(pl.multiple_of(j * 256, 256), 256)
        projected = jnp.dot(rows, w_buf[:, cols], preferred_element_type=jnp.float32)
        out_ref[:, cols] = (hid_buf[:, cols].astype(jnp.float32) + gate_ref[:, cols] * projected).astype(jnp.bfloat16)
        return carry

    lax.fori_loop(0, 6, project, 0)
    for copy in sent:
        copy.wait_send()


def on_device(queries, key_tokens, value_tokens, hidden, out_weight, attn_gate):
    bf16, f32 = jnp.bfloat16, jnp.float32
    dma = pltpu.SemaphoreType.DMA
    anywhere = pl.BlockSpec(memory_space=pl.ANY)
    in_vmem = pl.BlockSpec(memory_space=pltpu.VMEM)
    n = HEADS_DEV
    return pl.pallas_call(
        kernel,
        out_shape=jax.ShapeDtypeStruct(hidden.shape, bf16),
        in_specs=[anywhere] * 5 + [in_vmem],
        out_specs=in_vmem,
        scratch_shapes=[
            pltpu.VMEM((n, 2, 2, RING, TOK, 2 * DH), bf16),
            pltpu.VMEM((n, RING, 2, TOK, DH), bf16),
            pltpu.VMEM((n, RING, 2 * TOK, DH), bf16),
            pltpu.VMEM((n, RING - 1, 2 * TOK, DH), bf16),
            pltpu.VMEM((n, RING, 8, 2 * TOK), f32),
            pltpu.VMEM((n, RING - 1, 8, 2 * TOK), f32),
            pltpu.VMEM((4 * n, TOK, DH), bf16),
            pltpu.VMEM((n, TOK, DH), bf16),
            pltpu.VMEM(out_weight.shape, bf16),
            pltpu.VMEM(hidden.shape, bf16),
            dma((n, 3)), dma((2,)), dma((n, 3)), dma((n, 3)),
            dma((n, 2, 3)), dma((n, 2, 3)), dma((n, 2, 3)), dma((n, 2, 3)),
            dma((n, 2)), dma((n, 2)), dma((n, 3)), dma((n, 3)), dma((n, 3)), dma((n, 3)),
            dma((n, 3)), dma((n, 3)),
        ],
        compiler_params=pltpu.CompilerParams(
            collective_id=0, has_side_effects=True, vmem_limit_bytes=56 << 20
        ),
        cost_estimate=pl.CostEstimate(flops=15_000_000_000, bytes_accessed=8_000_000, transcendentals=14_000_000),
    )(queries, key_tokens, value_tokens, hidden, out_weight, attn_gate.reshape(1, -1))


def solution(mesh):
    return jax.shard_map(
        on_device,
        mesh=mesh,
        in_specs=(P("ctx", "grp"), P("ctx", "grp"), P("ctx", "grp"), P("ctx", None), P(), P()),
        out_specs=P("ctx", None),
        check_vma=False,
    )
```

time: 365 us -> 67.3 us (0.18)
  waiting for transfers between devices: 212 us -> 0 us
  matrix products: 65.2 us -> 0 us
  Pallas kernels: 0 us -> 63.9 us
  local copies, waits for them, and re-layouts: 50.6 us -> 3.21 us
  other arithmetic: 22 us -> 0 us
  between operations: 13.2 us -> 0.01 us
    all_gather x2 -> x0, waiting for transfers between devices: 177 us -> none  [the longest x1 116 us: on_device(): lax.all_gather(key_tokens, 'ctx', axis=0, tiled=True)]
    dot_general x5 -> x0, matrix products: 65.2 us -> none  [the longest x2 34.2 us: on_device(): jnp.einsum('hts,shd->thd', weights.astype(jnp.bfloat16), value_heads[:, l...]
    pallas_call x0 -> x1, Pallas kernels: none -> 63.9 us  [on_device(): pl.pallas_call(kernel, out_shape=jax.ShapeDtypeStruct(hidden.shape, bf16)...]
    all_gather x2 -> x0, local copies, waits for them, and re-layouts: 49.2 us -> none  [the longest x1 24.7 us: on_device(): lax.all_gather(key_tokens, 'ctx', axis=0, tiled=True)]
    psum x1 -> x0, waiting for transfers between devices: 34.2 us -> none  [on_device(): lax.psum(partial_proj.astype(jnp.bfloat16), 'grp').astype(jnp.float32)]
    reduce_sum x1 -> x0, other arithmetic: 19.9 us -> none  [on_device(): mass_parts.append(jnp.sum(weights, axis=-1))]
  transfers between devices with their start and end apart: 3 -> 0, of which waited for: 3 -> 0; matrix products, arithmetic and copies ran while one was open for 15% -> 0% of each run, Pallas kernels for 0% -> 0%
where the time goes in v1:
time: 67.3 us; the launch traced here: 67.1 us
  Pallas kernels  63.9 us (95%)
  local copies, waits for them, and re-layouts  3.21 us (5%)
    pallas_call x1, Pallas kernels, on_device(): pl.pallas_call(kernel, out_shape=jax.ShapeDtypeStruct(hidden.shape, bf16)...  63.9 us
    unnamed x1, local copies, waits for them, and re-layouts  1.92 us

profile of v1, /device:TPU:1, one launch (start us, length us, event | category | flops | bytes accessed | tf_op | source)
XLA Modules:
  0.0 67.1 jit_solution(9942444923619293925)
XLA Ops:
  0.0 1.3 %reshape.3.gate_ref = f32[1,1536]{1,0:T(1,128)} reshape(f32[1536]{0:T(1024)} %param.11) | data formatting | bytes 12288 | tf_op jit(solution)/shard_map/reshape | solution.py:278
  1.3 63.9 %shard_map.64 = bf16[192,1536]{1,0:T(8,128)(2,1)} custom-call(bf16[192,768]{1,0:T(8,128)(2,1)} %q_in.1, bf16[192,768]{1,0:T(8,128)(2,1)} %k_in.1, bf16[192,768]{1,0:T(8,128)(2,1)} %v_in.1, bf16[192,1536]{1,0:T(8,128)(2,1)} %hidden_in.1, bf16[1536,1536]{1,0:T(8,128)(2,1)} %w_in.1, f32[1,1536]{1,0:T(1,128)} %reshape.3.gate_ref), custom_call_target="tpu_custom_call" | custom-call | flops 15000000512 | bytes 8000000 | tf_op jit(solution)/shard_map/pallas_call | solution.py:253
  65.2 1.9 %copy.8 = bf16[192,1536]{1,0:T(8,128)(2,1)} copy(bf16[192,1536]{1,0:T(8,128)(2,1)} %shard_map.64) | data formatting | bytes 1179648

commit v2 on v1

v2 whole, which is shorter than its diff:
```python
import jax
import jax.numpy as jnp
from jax import lax
from jax.experimental import pallas as pl
from jax.experimental.pallas import tpu as pltpu
from jax.sharding import PartitionSpec as P

DH = 128
TOK = 192
HEADS_DEV = 3
RING = 4
SCALE = DH**-0.5 * 1.4426950408889634
NT = (((1,), (1,)), ((), ()))
NN = (((1,), (0,)), ((), ()))
MESH = pl.DeviceIdType.MESH
KV_AXIS = ("y", "z", "z")
Q_AXIS = ("z", "y", "y")
RELAYED = (False, True, True)
HALF = TOK // 2


def kernel(
    q_in, k_in, v_in, hidden_in, w_in, gate_in, out_hbm,
    kv, qb, o_send, o_recv, s_send, s_recv, att, a_send, w_buf, hid_buf, proj, top_buf, mix_buf, gate_ref, out_ref, x_kv_buf, x_q_buf,
    loc_sem, stage_sem, big_sem, x_send, x_recv, kv_send, kv_recv, q_send, q_recv,
    f_send, f_recv, r_send, r_recv, o_ssem, o_rsem, s_ssem, s_rsem, a_ssem, a_rsem,
):
    g = lax.axis_index("grp")
    t = lax.axis_index("ctx")
    core = t % 2
    place = {"xh": t // 32, "y": (t // 8) % 4, "z": (t // 2) % 4, "core": core}
    xh = place["xh"]

    def device(grp=None, **moved):
        at = dict(place, **moved)
        ctx = ((at["xh"] * 4 + at["y"]) * 4 + at["z"]) * 2 + at["core"]
        return (g if grp is None else grp, ctx)

    def ring(axis, step):
        return device(**{axis: (place[axis] + step) % RING})

    sibling = device(core=1 - core)
    x_partner = device(xh=1 - xh)
    x_kinds = (device(grp=1 - g), x_partner, device(grp=1 - g, xh=1 - xh))

    def columns(half, h):
        return pl.ds(pl.multiple_of((half * HEADS_DEV + h) * DH, DH), DH)

    def remote(src, dst, send, recv, to):
        return pltpu.make_async_remote_copy(
            src_ref=src, dst_ref=dst, send_sem=send, recv_sem=recv, device_id=to, device_id_type=MESH
        )

    own, stage = [], []
    for h in range(HEADS_DEV):
        cols = columns(xh, h)
        own.append((
            pltpu.make_async_copy(k_in.at[:, cols], kv.at[h, 0, 0, 0, :, pl.ds(0, DH)], loc_sem.at[h, 0]),
            pltpu.make_async_copy(v_in.at[:, cols], kv.at[h, 0, 0, 0, :, pl.ds(DH, DH)], loc_sem.at[h, 1]),
            pltpu.make_async_copy(q_in.at[:, cols], qb.at[h, 0, 0], loc_sem.at[h, 2]),
        ))
        cols = columns(1 - xh, h)
        stage.append((
            pltpu.make_async_copy(k_in.at[:, cols], x_kv_buf.at[h, :, pl.ds(0, DH)], stage_sem.at[h, 0]),
            pltpu.make_async_copy(v_in.at[:, cols], x_kv_buf.at[h, :, pl.ds(DH, DH)], stage_sem.at[h, 1]),
            pltpu.make_async_copy(q_in.at[:, cols], x_q_buf.at[h], stage_sem.at[h, 2]),
        ))
        for copy in (*stage[h], *own[h]):
            copy.start()
    w_copy = pltpu.make_async_copy(w_in, w_buf, big_sem.at[0])
    hid_copy = pltpu.make_async_copy(hidden_in, hid_buf, big_sem.at[1])
    gate_copy = pltpu.make_async_copy(gate_in, gate_ref, big_sem.at[2])

    barrier = pltpu.get_barrier_semaphore()
    peers = [ring(a, s) for a in ("y", "z") for s in (1, 2, 3)] + [sibling, *x_kinds]
    for peer in peers:
        pl.semaphore_signal(barrier, inc=1, device_id=peer, device_id_type=MESH)
    pl.semaphore_wait(barrier, len(peers))

    sent = []

    def start(copy):
        copy.start()
        sent.append(copy)

    def x_query(h):
        return remote(x_q_buf.at[h], qb.at[h, 0, 1], x_send.at[h, 0], x_recv.at[h, 0], x_partner)

    def x_kv(h):
        return remote(x_kv_buf.at[h], kv.at[h, 0, 1, 0], x_send.at[h, 1], x_recv.at[h, 1], x_partner)

    def kv_copy(h, xr, step):
        slot = RING - step
        return remote(
            kv.at[h, 0, xr, 0], kv.at[h, 0, xr, slot],
            kv_send.at[h, xr, slot - 1], kv_recv.at[h, xr, slot - 1], ring(KV_AXIS[h], step),
        )

    def q_copy(h, xr, step):
        slot = RING - step
        return remote(
            qb.at[h, 0, xr], qb.at[h, slot, xr],
            q_send.at[h, xr, slot - 1], q_recv.at[h, xr, slot - 1], ring(Q_AXIS[h], step),
        )

    def push_queries(h, xr):
        for step in (2, 1, 3):
            start(q_copy(h, xr, step))

    def push_kv(h, xr):
        for step in (1, 3) if RELAYED[h] else (2, 1, 3):
            start(kv_copy(h, xr, step))

    def relay_copy(h, xr, step):
        slot = RING - step
        rows = pl.ds(0 if step == 1 else HALF, HALF)
        n = 0 if step == 1 else 1
        return remote(
            kv.at[h, 0, xr, slot, rows], kv.at[h, 0, xr, 2, rows],
            r_send.at[h, xr, n], r_recv.at[h, xr, n], ring(KV_AXIS[h], step),
        )

    def relay(h, xr):
        for step in (1, 3):
            kv_copy(h, xr, step).wait_recv()
            start(relay_copy(h, xr, step))

    def forward_copy(h, xr):
        return remote(kv.at[h, 0, xr], kv.at[h, 1, xr], f_send.at[h, xr], f_recv.at[h, xr], sibling)

    def gathered(h, xr):
        if RELAYED[h]:
            for step in (1, 3):
                relay_copy(h, xr, step).wait_recv()
        else:
            for step in (1, 2, 3):
                kv_copy(h, xr, step).wait_recv()
        start(forward_copy(h, xr))

    def ready(h, xr):
        forward_copy(h, xr).wait_recv()

    def queries_ready(h):
        for xr in range(2):
            for step in (1, 2, 3):
                q_copy(h, xr, step).wait_recv()

    def o_copies(h, d):
        slot = RING - d
        to = ring(Q_AXIS[h], d)
        return (
            remote(o_send.at[h, d], o_recv.at[h, slot - 1], o_ssem.at[h, slot - 1], o_rsem.at[h, slot - 1], to),
            remote(s_send.at[h, d], s_recv.at[h, slot - 1], s_ssem.at[h, slot - 1], s_rsem.at[h, slot - 1], to),
        )

    def attend(rows, blocks, begin=True, end=True):
        items = [(row, block) for row in rows for block in blocks]
        stacked = {}
        for h, d in rows:
            scaled = qb[h, d].reshape(2 * TOK, DH).astype(jnp.float32) * SCALE
            high = scaled.astype(jnp.bfloat16)
            low = (scaled - high.astype(jnp.float32)).astype(jnp.bfloat16)
            stacked[h, d] = jnp.concatenate([high, low], axis=1)

        def scores(item):
            row, (cs, xr) = item
            keys = kv[row[0], cs, xr, :, :, :DH].reshape(RING * TOK, DH)
            return lax.dot_general(
                stacked[row], jnp.concatenate([keys, keys], axis=1), NT, preferred_element_type=jnp.float32
            )

        state = {}
        if not begin:
            for h, d in rows:
                state[h, d] = (top_buf[h, d - 1], mix_buf[h, d - 1])
        ahead = scores(items[0])
        for n, (row, (cs, xr)) in enumerate(items):
            now = ahead
            if n + 1 < len(items):
                ahead = scores(items[n + 1])
            values = kv[row[0], cs, xr, :, :, DH:].reshape(RING * TOK, DH)
            top = jnp.max(now, axis=1, keepdims=True)
            if row in state:
                top = jnp.maximum(top, state[row][0])
            weights = jnp.exp2(now - top).astype(jnp.bfloat16)
            mixed = lax.dot_general(
                weights, jnp.concatenate([values, jnp.ones_like(values)], axis=1), NN,
                preferred_element_type=jnp.float32,
            )
            if row in state:
                mixed = mixed + state[row][1] * jnp.exp2(state[row][0] - top)
            state[row] = (top, mixed)
        for h, d in rows:
            top, mixed = state[h, d]
            if end:
                mass = mixed[:, DH:]
                o_send[h, d] = (mixed[:, :DH] / mass).astype(jnp.bfloat16)
                s_send[h, d] = jnp.transpose(top + jnp.log2(mass))[:8]
            else:
                top_buf[h, d - 1] = top
                mix_buf[h, d - 1] = mixed
        for h, d in rows:
            if end and d:
                for copy in o_copies(h, d):
                    start(copy)

    def a_copies(h):
        at = (g * 2 + xh) * HEADS_DEV + h
        return [
            remote(att.at[at] if kind == 0 else a_send.at[h], att.at[at], a_ssem.at[h, kind], a_rsem.at[h, kind], x_kinds[kind])
            for kind in range(3)
        ]

    def a_arrivals(h):
        places = ((1 - g) * 2 + xh, g * 2 + 1 - xh, (1 - g) * 2 + 1 - xh)
        return [
            remote(a_send.at[h], att.at[places[kind] * HEADS_DEV + h], a_ssem.at[h, kind], a_rsem.at[h, kind], x_kinds[kind])
            for kind in range(3)
        ]

    def combine(h):
        for d in (1, 2, 3):
            for copy in o_copies(h, d):
                copy.wait_recv()
        sums = [s_send[h, 0]] + [s_recv[h, j] for j in range(3)]
        parts = [o_send[h, 0]] + [o_recv[h, j] for j in range(3)]
        top = jnp.maximum(jnp.maximum(sums[0], sums[1]), jnp.maximum(sums[2], sums[3]))
        shares = [jnp.exp2(s - top) for s in sums]
        total = (shares[0] + shares[1]) + (shares[2] + shares[3])
        whole = None
        for share, part in zip(shares, parts):
            by_row = jnp.transpose(jnp.broadcast_to((share / total)[:1], (DH, 2 * TOK)))
            term = by_row * part.astype(jnp.float32)
            whole = term if whole is None else whole + term
        whole = whole.astype(jnp.bfloat16)
        att[(g * 2 + xh) * HEADS_DEV + h] = whole[:TOK]
        a_send[h] = whole[TOK:]
        for copy in a_copies(h):
            start(copy)

    def project(h, first):
        places = [k * HEADS_DEV + h for k in range(4)]
        rows = jnp.concatenate([att[p] for p in places], axis=1)
        for n in range(0, w_buf.shape[1], 512):
            weight = jnp.concatenate([w_buf[p * DH : (p + 1) * DH, n : n + 512] for p in places], axis=0)
            part = jnp.dot(rows, weight, preferred_element_type=jnp.float32)
            proj[:, n : n + 512] = part if first else proj[:, n : n + 512] + part

    def wait_attended(h):
        for copy in a_arrivals(h):
            copy.wait_recv()

    def remote_rows(h):
        return [(h, d) for d in (1, 3, 2)]

    def start_all(copies):
        for copy in copies:
            start(copy)

    def wait_own(h):
        for copy in own[h]:
            copy.wait()

    def wait_staged(h):
        for copy in stage[h]:
            copy.wait()

    def partner_queries(h):
        x_query(h).wait_recv()
        push_queries(h, 1)

    def partner_kv(h):
        x_kv(h).wait_recv()
        push_kv(h, 1)

    wait_staged(0)
    start(x_query(0))
    wait_own(0)
    push_queries(0, 0)
    push_kv(0, 0)
    wait_staged(1)
    start(x_query(1))
    start(x_kv(0))
    wait_own(1)
    push_kv(1, 0)
    push_queries(1, 0)
    start(x_kv(1))
    wait_staged(2)
    start(x_query(2))
    start(x_kv(2))
    partner_queries(0)
    partner_queries(1)
    partner_kv(0)
    wait_own(2)
    push_kv(2, 0)
    push_queries(2, 0)
    w_copy.start()
    hid_copy.start()
    gate_copy.start()
    relay(1, 0)
    gathered(0, 0)
    queries_ready(0)
    first, second, third = ([(h, d) for d in (1, 3, 2)] for h in range(HEADS_DEV))
    attend(first, [(0, 0)], end=False)
    partner_kv(1)
    ready(0, 0)
    attend(first, [(1, 0)], begin=False, end=False)
    relay(2, 0)
    partner_queries(2)
    partner_kv(2)
    gathered(1, 0)
    queries_ready(1)
    attend(second, [(0, 0)], end=False)
    relay(1, 1)
    ready(1, 0)
    attend(second, [(1, 0)], begin=False, end=False)
    gathered(0, 1)
    attend(first, [(0, 1)], begin=False, end=False)
    relay(2, 1)
    gathered(1, 1)
    ready(0, 1)
    attend(first, [(1, 1)], begin=False)
    gathered(2, 0)
    ready(1, 1)
    attend(second, [(0, 1), (1, 1)], begin=False)
    gathered(2, 1)
    queries_ready(2)
    ready(2, 0)
    attend(third, [(0, 0), (1, 0)], end=False)
    ready(2, 1)
    attend(third, [(0, 1), (1, 1)], begin=False)
    every = [(0, 0), (0, 1), (1, 0), (1, 1)]
    attend([(0, 0), (1, 0)], every)
    combine(0)
    combine(1)
    attend([(2, 0)], every)
    combine(2)
    w_copy.wait()
    hid_copy.wait()
    gate_copy.wait()
    for copy in sent[:-3]:
        copy.wait_send()
    for h in range(HEADS_DEV):
        wait_attended(h)
        project(h, h == 0)
    out_copies = []
    for n in range(2):
        rows = pl.ds(n * HALF, HALF)
        out_ref[rows] = (
            hid_buf[rows].astype(jnp.float32) + gate_ref[...].reshape(1, -1) * proj[rows]
        ).astype(jnp.bfloat16)
        out_copies.append(pltpu.make_async_copy(out_ref.at[rows], out_hbm.at[rows], big_sem.at[3 + n]))
        out_copies[n].start()
    for copy in sent[-3:]:
        copy.wait_send()
    for copy in out_copies:
        copy.wait()


def on_device(queries, key_tokens, value_tokens, hidden, out_weight, attn_gate):
    bf16, f32 = jnp.bfloat16, jnp.float32
    dma = pltpu.SemaphoreType.DMA
    anywhere = pl.BlockSpec(memory_space=pl.ANY)
    n = HEADS_DEV
    return pl.pallas_call(
        kernel,
        out_shape=jax.ShapeDtypeStruct(hidden.shape, bf16),
        in_specs=[anywhere] * 6,
        out_specs=anywhere,
        scratch_shapes=[
            pltpu.VMEM((n, 2, 2, RING, TOK, 2 * DH), bf16),
            pltpu.VMEM((n, RING, 2, TOK, DH), bf16),
            pltpu.VMEM((n, RING, 2 * TOK, DH), bf16),
            pltpu.VMEM((n, RING - 1, 2 * TOK, DH), bf16),
            pltpu.VMEM((n, RING, 8, 2 * TOK), f32),
            pltpu.VMEM((n, RING - 1, 8, 2 * TOK), f32),
            pltpu.VMEM((4 * n, TOK, DH), bf16),
            pltpu.VMEM((n, TOK, DH), bf16),
            pltpu.VMEM(out_weight.shape, bf16),
            pltpu.VMEM(hidden.shape, bf16),
            pltpu.VMEM(hidden.shape, f32),
            pltpu.VMEM((n, RING - 1, 2 * TOK, 1), f32),
            pltpu.VMEM((n, RING - 1, 2 * TOK, 2 * DH), f32),
            pltpu.VMEM(attn_gate.shape, f32),
            pltpu.VMEM(hidden.shape, bf16),
            pltpu.VMEM((n, TOK, 2 * DH), bf16),
            pltpu.VMEM((n, TOK, DH), bf16),
            dma((n, 3)), dma((n, 3)), dma((5,)), dma((n, 2)), dma((n, 2)),
            dma((n, 2, 3)), dma((n, 2, 3)), dma((n, 2, 3)), dma((n, 2, 3)),
            dma((n, 2)), dma((n, 2)), dma((n, 2, 2)), dma((n, 2, 2)), dma((n, 3)), dma((n, 3)), dma((n, 3)), dma((n, 3)),
            dma((n, 3)), dma((n, 3)),
        ],
        compiler_params=pltpu.CompilerParams(
            collective_id=0, has_side_effects=True, vmem_limit_bytes=56 << 20
        ),
        cost_estimate=pl.CostEstimate(flops=15_000_000_000, bytes_accessed=8_000_000, transcendentals=14_000_000),
    )(queries, key_tokens, value_tokens, hidden, out_weight, attn_gate)


def solution(mesh):
    return jax.shard_map(
        on_device,
        mesh=mesh,
        in_specs=(P("ctx", "grp"), P("ctx", "grp"), P("ctx", "grp"), P("ctx", None), P(), P()),
        out_specs=P("ctx", None),
        check_vma=False,
    )
```

time: 67.3 us -> 52.7 us (0.78)
  Pallas kernels: 63.9 us -> 50.3 us
  local copies, waits for them, and re-layouts: 3.21 us -> 1.92 us
    pallas_call x1, Pallas kernels: 63.9 us -> 50.3 us  [on_device(): pl.pallas_call(kernel, out_shape=jax.ShapeDtypeStruct(hidden.shape, bf16)...]
    reshape x1 -> x0, local copies, waits for them, and re-layouts: 1.29 us -> none  [on_device(): attn_gate.reshape(1, -1)]
where the time goes in v2:
time: 52.7 us; the launch traced here: 52.2 us
  Pallas kernels  50.3 us (95%)
  local copies, waits for them, and re-layouts  1.92 us (4%)
    pallas_call x1, Pallas kernels, on_device(): pl.pallas_call(kernel, out_shape=jax.ShapeDtypeStruct(hidden.shape, bf16)...  50.3 us
    unnamed x1, local copies, waits for them, and re-layouts  1.92 us

profile of v2, /device:TPU:1, one launch (start us, length us, event | category | flops | bytes accessed | tf_op | source)
XLA Modules:
  0.0 52.2 jit_solution(12103752227438329447)
XLA Ops:
  0.0 50.3 %shard_map.64 = bf16[192,1536]{1,0:T(8,128)(2,1)} custom-call(bf16[192,768]{1,0:T(8,128)(2,1)} %q_in.1, bf16[192,768]{1,0:T(8,128)(2,1)} %k_in.1, bf16[192,768]{1,0:T(8,128)(2,1)} %v_in.1, bf16[192,1536]{1,0:T(8,128)(2,1)} %hidden_in.1, bf16[1536,1536]{1,0:T(8,128)(2,1)} %w_in.1, f32[1536]{0:T(1024)} %gate_in.1), custom_call_target="tpu_custom_call" | custom-call | flops 15000000512 | bytes 8000000 | tf_op jit(solution)/shard_map/pallas_call | solution.py:365
  50.3 1.9 %copy.8 = bf16[192,1536]{1,0:T(8,128)(2,1)} copy(bf16[192,1536]{1,0:T(8,128)(2,1)} %shard_map.64) | data formatting | bytes 1179648

commit v3 on v2

--- a/solution.py
+++ b/solution.py
@@ -20,8 +20,8 @@
 
 
 def kernel(
-    q_in, k_in, v_in, hidden_in, w_in, gate_in, out_hbm,
-    kv, qb, o_send, o_recv, s_send, s_recv, att, a_send, w_buf, hid_buf, proj, top_buf, mix_buf, gate_ref, out_ref, x_kv_buf, x_q_buf,
+    q_in, k_in, v_in, hidden_in, w_in, gate_in, out_ref,
+    kv, qb, o_send, o_recv, s_send, s_recv, att, a_send, w_buf, hid_buf, proj, top_buf, mix_buf, gate_ref, x_kv_buf, x_q_buf,
     loc_sem, stage_sem, big_sem, x_send, x_recv, kv_send, kv_recv, q_send, q_recv,
     f_send, f_recv, r_send, r_recv, o_ssem, o_rsem, s_ssem, s_rsem, a_ssem, a_rsem,
 ):
@@ -50,6 +50,11 @@
         return pltpu.make_async_remote_copy(
             src_ref=src, dst_ref=dst, send_sem=send, recv_sem=recv, device_id=to, device_id_type=MESH
         )
+
+    barrier = pltpu.get_barrier_semaphore()
+    peers = [ring(a, s) for a in ("y", "z") for s in (1, 2, 3)] + [sibling, *x_kinds]
+    for peer in peers:
+        pl.semaphore_signal(barrier, inc=1, device_id=peer, device_id_type=MESH)
 
     own, stage = [], []
     for h in range(HEADS_DEV):
@@ -71,10 +76,6 @@
     hid_copy = pltpu.make_async_copy(hidden_in, hid_buf, big_sem.at[1])
     gate_copy = pltpu.make_async_copy(gate_in, gate_ref, big_sem.at[2])
 
-    barrier = pltpu.get_barrier_semaphore()
-    peers = [ring(a, s) for a in ("y", "z") for s in (1, 2, 3)] + [sibling, *x_kinds]
-    for peer in peers:
-        pl.semaphore_signal(barrier, inc=1, device_id=peer, device_id_type=MESH)
     pl.semaphore_wait(barrier, len(peers))
 
     sent = []
@@ -265,6 +266,13 @@
         for copy in stage[h]:
             copy.wait()
 
+    def push_own(h):
+        steps = (1, 3) if RELAYED[h] else (2, 1, 3)
+        for step in (2, 1, 3):
+            start(q_copy(h, 0, step))
+            if step in steps:
+                start(kv_copy(h, 0, step))
+
     def partner_queries(h):
         x_query(h).wait_recv()
         push_queries(h, 1)
@@ -273,27 +281,21 @@
         x_kv(h).wait_recv()
         push_kv(h, 1)
 
-    wait_staged(0)
+    for h in range(HEADS_DEV):
+        wait_staged(h)
+        wait_own(h)
     start(x_query(0))
-    wait_own(0)
-    push_queries(0, 0)
-    push_kv(0, 0)
-    wait_staged(1)
+    push_own(0)
     start(x_query(1))
     start(x_kv(0))
-    wait_own(1)
-    push_kv(1, 0)
-    push_queries(1, 0)
+    push_own(1)
+    partner_queries(0)
     start(x_kv(1))
-    wait_staged(2)
+    partner_queries(1)
     start(x_query(2))
+    partner_kv(0)
     start(x_kv(2))
-    partner_queries(0)
-    partner_queries(1)
-    partner_kv(0)
-    wait_own(2)
-    push_kv(2, 0)
-    push_queries(2, 0)
+    push_own(2)
     w_copy.start()
     hid_copy.start()
     gate_copy.start()
@@ -343,18 +345,11 @@
     for h in range(HEADS_DEV):
         wait_attended(h)
         project(h, h == 0)
-    out_copies = []
-    for n in range(2):
-        rows = pl.ds(n * HALF, HALF)
-        out_ref[rows] = (
-            hid_buf[rows].astype(jnp.float32) + gate_ref[...].reshape(1, -1) * proj[rows]
-        ).astype(jnp.bfloat16)
-        out_copies.append(pltpu.make_async_copy(out_ref.at[rows], out_hbm.at[rows], big_sem.at[3 + n]))
-        out_copies[n].start()
+    out_ref[...] = (
+        hid_buf[...].astype(jnp.float32) + gate_ref[...].reshape(1, -1) * proj[...]
+    ).astype(jnp.bfloat16)
     for copy in sent[-3:]:
         copy.wait_send()
-    for copy in out_copies:
-        copy.wait()
 
 
 def on_device(queries, key_tokens, value_tokens, hidden, out_weight, attn_gate):
@@ -364,9 +359,9 @@
     n = HEADS_DEV
     return pl.pallas_call(
         kernel,
-        out_shape=jax.ShapeDtypeStruct(hidden.shape, bf16),
+        out_shape=pltpu.VMEM(hidden.shape, bf16),
         in_specs=[anywhere] * 6,
-        out_specs=anywhere,
+        out_specs=pl.BlockSpec(memory_space=pltpu.VMEM),
         scratch_shapes=[
             pltpu.VMEM((n, 2, 2, RING, TOK, 2 * DH), bf16),
             pltpu.VMEM((n, RING, 2, TOK, DH), bf16),
@@ -382,10 +377,9 @@
             pltpu.VMEM((n, RING - 1, 2 * TOK, 1), f32),
             pltpu.VMEM((n, RING - 1, 2 * TOK, 2 * DH), f32),
             pltpu.VMEM(attn_gate.shape, f32),
-            pltpu.VMEM(hidden.shape, bf16),
             pltpu.VMEM((n, TOK, 2 * DH), bf16),
             pltpu.VMEM((n, TOK, DH), bf16),
-            dma((n, 3)), dma((n, 3)), dma((5,)), dma((n, 2)), dma((n, 2)),
+            dma((n, 3)), dma((n, 3)), dma((3,)), dma((n, 2)), dma((n, 2)),
             dma((n, 2, 3)), dma((n, 2, 3)), dma((n, 2, 3)), dma((n, 2, 3)),
             dma((n, 2)), dma((n, 2)), dma((n, 2, 2)), dma((n, 2, 2)), dma((n, 3)), dma((n, 3)), dma((n, 3)), dma((n, 3)),
             dma((n, 3)), dma((n, 3)),

time: 52.7 us -> 50.8 us (0.964)
  local copies, waits for them, and re-layouts: 1.92 us -> 0.82 us
  Pallas kernels: 50.3 us -> 49.6 us
    unnamed x1, local copies, waits for them, and re-layouts: 1.92 us -> 0.82 us
    pallas_call x1, Pallas kernels: 50.3 us -> 49.6 us  [on_device(): pl.pallas_call(kernel, out_shape=pltpu.VMEM(hidden.shape, bf16), in_specs...]
where the time goes in v3:
time: 50.8 us; the launch traced here: 50.4 us
  Pallas kernels  49.6 us (98%)
  local copies, waits for them, and re-layouts  0.82 us (2%)
    pallas_call x1, Pallas kernels, on_device(): pl.pallas_call(kernel, out_shape=pltpu.VMEM(hidden.shape, bf16), in_specs...  49.6 us

profile of v3, /device:TPU:1, one launch (start us, length us, event | category | flops | bytes accessed | tf_op | source)
XLA Modules:
  0.0 50.4 jit_solution(12090000045283248062)
XLA Ops:
  0.0 49.6 %shard_map.64 = bf16[192,1536]{1,0:T(8,128)(2,1)S(1)} custom-call(bf16[192,768]{1,0:T(8,128)(2,1)} %q_in.1, bf16[192,768]{1,0:T(8,128)(2,1)} %k_in.1, bf16[192,768]{1,0:T(8,128)(2,1)} %v_in.1, bf16[192,1536]{1,0:T(8,128)(2,1)} %hidden_in.1, bf16[1536,1536]{1,0:T(8,128)(2,1)} %w_in.1, f32[1536]{0:T(1024)} %gate_in.1), custom_call_target="tpu_custom_call" | custom-call | flops 15000000512 | bytes 8000000 | tf_op jit(solution)/shard_map/pallas_call | solution.py:360
  49.6 0.8 %copy.8 = bf16[192,1536]{1,0:T(8,128)(2,1)} copy(bf16[192,1536]{1,0:T(8,128)(2,1)S(1)} %shard_map.64) | data formatting | bytes 1179648

commit v4 on v3

--- a/solution.py
+++ b/solution.py
@@ -236,8 +236,9 @@
         whole = whole.astype(jnp.bfloat16)
         att[(g * 2 + xh) * HEADS_DEV + h] = whole[:TOK]
         a_send[h] = whole[TOK:]
-        for copy in a_copies(h):
-            start(copy)
+        copies = a_copies(h)
+        for kind in (1, 2, 0):
+            start(copies[kind])
 
     def project(h, first):
         places = [k * HEADS_DEV + h for k in range(4)]
@@ -332,11 +333,9 @@
     ready(2, 1)
     attend(third, [(0, 1), (1, 1)], begin=False)
     every = [(0, 0), (0, 1), (1, 0), (1, 1)]
-    attend([(0, 0), (1, 0)], every)
-    combine(0)
-    combine(1)
-    attend([(2, 0)], every)
-    combine(2)
+    for h in range(HEADS_DEV):
+        attend([(h, 0)], every)
+        combine(h)
     w_copy.wait()
     hid_copy.wait()
     gate_copy.wait()

time: 50.8 us -> 50.5 us (level)
  Pallas kernels: 49.6 us -> 49 us
    pallas_call x1, Pallas kernels: 49.6 us -> 49 us  [on_device(): pl.pallas_call(kernel, out_shape=pltpu.VMEM(hidden.shape, bf16), in_specs...]
where the time goes in v4:
time: 50.5 us; the launch traced here: 49.8 us
  Pallas kernels  49 us (97%)
  local copies, waits for them, and re-layouts  0.82 us (2%)
    pallas_call x1, Pallas kernels, on_device(): pl.pallas_call(kernel, out_shape=pltpu.VMEM(hidden.shape, bf16), in_specs...  49 us

profile of v4, /device:TPU:1, one launch (start us, length us, event | category | flops | bytes accessed | tf_op | source)
XLA Modules:
  0.0 49.8 jit_solution(9660755827174854024)
XLA Ops:
  0.0 49.0 %shard_map.64 = bf16[192,1536]{1,0:T(8,128)(2,1)S(1)} custom-call(bf16[192,768]{1,0:T(8,128)(2,1)} %q_in.1, bf16[192,768]{1,0:T(8,128)(2,1)} %k_in.1, bf16[192,768]{1,0:T(8,128)(2,1)} %v_in.1, bf16[192,1536]{1,0:T(8,128)(2,1)} %hidden_in.1, bf16[1536,1536]{1,0:T(8,128)(2,1)} %w_in.1, f32[1536]{0:T(1024)} %gate_in.1), custom_call_target="tpu_custom_call" | custom-call | flops 15000000512 | bytes 8000000 | tf_op jit(solution)/shard_map/pallas_call | solution.py:359
  49.0 0.8 %copy.8 = bf16[192,1536]{1,0:T(8,128)(2,1)} copy(bf16[192,1536]{1,0:T(8,128)(2,1)S(1)} %shard_map.64) | data formatting | bytes 1179648

commit v5 on v4

--- a/solution.py
+++ b/solution.py
@@ -200,7 +200,7 @@
             else:
                 top_buf[h, d - 1] = top
                 mix_buf[h, d - 1] = mixed
-        for h, d in rows:
+        for h, d in sorted(rows, key=lambda row: row[1] != 2):
             if end and d:
                 for copy in o_copies(h, d):
                     start(copy)

time: 50.5 us -> 50.5 us (level); the launches traced: 49.8 us -> 50.4 us
  Pallas kernels: 49 us -> 49.6 us
    pallas_call x1, Pallas kernels: 49 us -> 49.6 us  [on_device(): pl.pallas_call(kernel, out_shape=pltpu.VMEM(hidden.shape, bf16), in_specs...]
where the time goes in v5:
time: 50.5 us; the launch traced here: 50.4 us
  Pallas kernels  49.6 us (98%)
  local copies, waits for them, and re-layouts  0.82 us (2%)
    pallas_call x1, Pallas kernels, on_device(): pl.pallas_call(kernel, out_shape=pltpu.VMEM(hidden.shape, bf16), in_specs...  49.6 us

profile of v5, /device:TPU:1, one launch (start us, length us, event | category | flops | bytes accessed | tf_op | source)
XLA Modules:
  0.0 50.4 jit_solution(289585851476700212)
XLA Ops:
  0.0 49.6 %shard_map.64 = bf16[192,1536]{1,0:T(8,128)(2,1)S(1)} custom-call(bf16[192,768]{1,0:T(8,128)(2,1)} %q_in.1, bf16[192,768]{1,0:T(8,128)(2,1)} %k_in.1, bf16[192,768]{1,0:T(8,128)(2,1)} %v_in.1, bf16[192,1536]{1,0:T(8,128)(2,1)} %hidden_in.1, bf16[1536,1536]{1,0:T(8,128)(2,1)} %w_in.1, f32[1536]{0:T(1024)} %gate_in.1), custom_call_target="tpu_custom_call" | custom-call | flops 15000000512 | bytes 8000000 | tf_op jit(solution)/shard_map/pallas_call | solution.py:359
  49.6 0.8 %copy.8 = bf16[192,1536]{1,0:T(8,128)(2,1)} copy(bf16[192,1536]{1,0:T(8,128)(2,1)S(1)} %shard_map.64) | data formatting | bytes 1179648
